TPU v7x, 256 devices: a whole 4x4x8 slice. The times are simulated.
256 devices in a mesh: dp: 8 (over z), row: 16 (over y, x), col: 2 (over core).
Axes of the slice: x: 4, y: 4, z: 8, core: 2. Of those that a mesh axis runs over, the one named last changes fastest.
Arguments:
- inputs: bfloat16 [4096, 8192], P('dp', 'row'), may hold values from -6 to 6
- frozen: bfloat16 [8192, 14336], P('row', 'col'), may hold values from -0.0625 to 0.0625
- factor_b: bfloat16 [8192, 64], P('row'), may hold values from -0.0625 to 0.0625
- factor_a: bfloat16 [64, 14336], P(None, 'col'), may hold values from -0.75 to 0.75
- magnitude: float32 [14336], P('col'), may hold values from 0.5 to 2
- cotangent: bfloat16 [4096, 14336], P('dp', 'col'), may hold values from -6 to 6
Outputs:
- mixed: bfloat16 [4096, 14336], P(('dp', 'row'), 'col')
- input_grad: bfloat16 [4096, 8192], P('dp', ('row', 'col'))
- a_grad: float32 [64, 14336], P(None, 'col')
- b_grad: float32 [8192, 64], P('row')
- magnitude_grad: float32 [14336], P('col')
All inputs are finite; a program needn't handle non-finite values.
Results may differ from a plain program's by a relative error of at most 0.0055.
Values may be sent and summed in bfloat16 or wider, within the bound.
A program may use at most 128 MiB of HBM per device.

v0:
```python
import jax
import jax.numpy as jnp
from jax import lax
from jax.sharding import PartitionSpec as P


def body(inputs, frozen, factor_b, factor_a, magnitude, cotangent):
    highest = lax.Precision.HIGHEST
    adapted = frozen.astype(jnp.float32) + jnp.dot(
        factor_b, factor_a, preferred_element_type=jnp.float32
    )
    column_square = lax.psum(jnp.sum(adapted * adapted, axis=0), "row")
    column_norm = jnp.sqrt(column_square + 1e-06)
    scale = magnitude / column_norm
    factor_wide = factor_a.astype(jnp.float32)
    proj_part = jnp.dot(inputs, factor_b, preferred_element_type=jnp.float32)
    row_index = lax.axis_index("row")
    token_share = inputs.shape[0] // lax.axis_size("row")
    start = row_index * token_share
    projected = lax.psum(proj_part, "row")
    term = jnp.dot(inputs, frozen, preferred_element_type=jnp.float32)
    pre_rows = lax.psum_scatter(term, "row", scatter_dimension=0, tiled=True)
    own_projected = lax.dynamic_slice_in_dim(projected, start, token_share, 0)
    pre_rows = pre_rows + jnp.dot(own_projected, factor_wide, precision=highest)
    mixed = (pre_rows * scale).astype(jnp.bfloat16)
    grad_rows = lax.dynamic_slice_in_dim(cotangent, start, token_share, 0).astype(jnp.float32)
    mag_part = jnp.sum(grad_rows * pre_rows, axis=0) / column_norm
    grad_pre = cotangent.astype(jnp.float32) * scale
    grad_low = grad_pre.astype(jnp.bfloat16)
    up_part = jnp.dot(grad_pre, factor_wide.T, precision=highest).astype(jnp.bfloat16)
    upstream = lax.psum(up_part, "col").astype(jnp.float32).astype(jnp.bfloat16)
    frozen_part = jnp.dot(grad_low, frozen.T, preferred_element_type=jnp.float32)
    frozen_sum = lax.psum_scatter(frozen_part, "col", scatter_dimension=1, tiled=True)
    col_share = factor_b.shape[0] // lax.axis_size("col")
    b_block = lax.dynamic_slice_in_dim(factor_b, lax.axis_index("col") * col_share, col_share, 0)
    input_grad = (
        frozen_sum + jnp.dot(upstream, b_block.T, preferred_element_type=jnp.float32)
    ).astype(jnp.bfloat16)
    b_part = jnp.dot(inputs.T, upstream, preferred_element_type=jnp.float32)
    a_part = jnp.dot(projected.T, grad_pre, precision=highest)
    a_grad, b_grad = lax.psum((a_part, b_part), "dp")
    magnitude_grad = lax.psum(mag_part, ("dp", "row"))
    return (mixed, input_grad, a_grad, b_grad, magnitude_grad)


def solution(mesh):
    return jax.shard_map(
        body,
        mesh=mesh,
        in_specs=(
            P("dp", "row"),
            P("row", "col"),
            P("row", None),
            P(None, "col"),
            P("col"),
            P("dp", "col"),
        ),
        out_specs=(
            P(("dp", "row"), "col"),
            P("dp", ("row", "col")),
            P(None, "col"),
            P("row", None),
            P("col"),
        ),
        check_vma=False,
    )
```

profile of v0, /device:TPU:4, one launch (start us, length us, event | category | flops | bytes accessed | tf_op | source)
XLA Modules:
  0.0 1045.5 jit_solution(2328476609069340265)
XLA Ops:
  7.2 0.0 all-reduce.7.cloned.1.call-start
  7.2 1.1 copy-done
  8.4 5.3 multiply_reduce_fusion
  13.7 70.5 %psum.43 = f32[7168]{0:T(1024)S(1)} all-reduce(f32[7168]{0:T(1024)S(1)} %multiply_reduce_fusion), channel_id=1, replica_groups=mesh['dp'=8,'row'=16,'col'=2] {'row'}, use_global_device_ids=true, to_apply=%region_3.0 | all-reduce | flops 7168 | bytes 57344 | tf_op jit(solution)/shard_map/psum | solution.py:12
  84.2 11.2 %fusion.9 = bf16[512,64]{0,1:T(8,128)(2,1)} fusion(bf16[64,7168]{1,0:T(8,128)(2,1)S(1)} %copy-done, bf16[512,7168]{1,0:T(8,128)(2,1)} %param.11, f32[7168]{0:T(1024)S(1)} %fusion.13), kind=kOutput, calls=%fused_computation.13 | convolution fusion | flops 2825945088 | bytes 8351744 | tf_op jit(solution)/shard_map/dot_general | solution.py:30
  95.4 0.0 all-reduce.7.cloned.1.call-update
  95.4 0.0 all-reduce.5.cloned.1.call-start
  95.5 0.9 fusion.17
  96.4 0.0 reduce-scatter.5.cloned.1.call-start
  96.5 10.1 fusion.3
  106.7 0.2 reduce-scatter.3.cloned.1.call-start
  106.9 10.4 fusion.16
  117.3 0.0 all-reduce.9.cloned.1.call-start
  117.4 8.8 all-reduce.7.cloned.1.call-done
  126.2 1.8 convolution_bitcast_fusion
  127.9 94.7 %all-reduce.5.cloned.1.call-done = f32[512,64]{0,1:T(8,128)} async-done(((f32[512,64]{0,1:T(8,128)}), f32[512,64]{0,1:T(8,128)}) %all-reduce.5.cloned.1.call-update) | async-done | bytes 131088 | tf_op jit(solution)/shard_map/psum | solution.py:20
  222.7 12.8 %fusion = f32[64,7168]{1,0:T(8,128)} fusion(f32[512,64]{0,1:T(8,128)} %all-reduce.5.cloned.1.call-done, bf16[512,7168]{1,0:T(8,128)(2,1)} %param.11, f32[7168]{0:T(1024)S(1)} %fusion.13), kind=kOutput, calls=%fused_computation.1 | convolution fusion | flops 2825912320 | bytes 9334784 | tf_op jit(solution)/shard_map/dot_general | solution.py:40
  235.5 4.1 reduce-scatter.5.cloned.1.call-done
  239.6 2.0 fusion.8
  241.6 108.5 %reduce-scatter.3.cloned.1.call-done = f32[32,7168]{1,0:T(8,128)} async-done(((f32[512,7168]{1,0:T(8,128)}), f32[32,7168]{1,0:T(8,128)}) %reduce-scatter.3.cloned.1.call-update) | async-done | bytes 917520 | tf_op jit(solution)/shard_map/reduce_scatter | solution.py:22
  350.1 2.9 multiply_reduce_fusion.1
  353.1 681.5 %psum.47 = f32[7168]{0:T(1024)} all-reduce(f32[7168]{0:T(1024)S(1)} %fusion.12), channel_id=1, replica_groups=mesh['dp'=8,'row'=16,'col'=2] {'dp','row'}, use_global_device_ids=true, to_apply=%region_9.0 | all-reduce | flops 7168 | bytes 57344 | tf_op jit(solution)/shard_map/psum | solution.py:42
  1034.6 2.9 copy.15
  1037.4 1.6 copy.16
  (16 shorter events, 0.1 us)
Async XLA Ops:
  7.2 1.2 copy-start
  7.2 77.0 %copy-start.4 = (f32[7168]{0:T(1024)S(1)}, f32[7168]{0:T(1024)}, u32[]{:S(2)}) copy-start(f32[7168]{0:T(1024)} %param.10) | copy-start | bytes 86020
  7.2 119.0 %all-reduce.7.cloned.1.call-start = ((), (), s32[]{:S(2)}) async-start(), calls=%async_computation.5 | async-start | bytes 131072 | tf_op jit(solution)/shard_map/psum | solution.py:31
  13.7 81.8 %copy-start.1 = (bf16[512,512]{1,0:T(8,128)(2,1)S(1)}, bf16[512,512]{1,0:T(8,128)(2,1)}, u32[]{:S(2)}) copy-start(bf16[512,512]{1,0:T(8,128)(2,1)} %param.6) | copy-start | bytes 1572868
  13.7 81.8 %copy-start.3 = (bf16[512,64]{0,1:T(8,128)(2,1)S(1)}, bf16[512,64]{0,1:T(8,128)(2,1)}, u32[]{:S(2)}) copy-start(bf16[512,64]{0,1:T(8,128)(2,1)} %param.8) | copy-start | bytes 196612
  95.4 127.2 %all-reduce.5.cloned.1.call-start = ((), (), s32[]{:S(2)}) async-start(), calls=%async_computation.3 | async-start | bytes 262144 | tf_op jit(solution)/shard_map/psum | solution.py:20
  96.4 143.2 %reduce-scatter.5.cloned.1.call-start = ((), (), s32[]{:S(2)}) async-start(), calls=%async_computation.4 | async-start | bytes 1572864 | tf_op jit(solution)/shard_map/reduce_scatter | solution.py:33
  106.7 243.5 %reduce-scatter.3.cloned.1.call-start = ((), (), s32[]{:S(2)}) async-start(), calls=%async_computation.2 | async-start | bytes 15597568 | tf_op jit(solution)/shard_map/reduce_scatter | solution.py:22
  117.3 917.2 %all-reduce.9.cloned.1.call-start = ((), (), s32[]{:S(2)}) async-start(), calls=%async_computation.6 | async-start | bytes 3932160 | tf_op jit(solution)/shard_map/psum | solution.py:41
  126.2 113.5 %copy-start.2 = (bf16[512,64]{0,1:T(8,128)(2,1)S(1)}, bf16[512,64]{0,1:T(8,128)(2,1)}, u32[]{:S(2)}) copy-start(bf16[512,64]{0,1:T(8,128)(2,1)} %all-reduce.7.cloned.1.call-done) | copy-start | bytes 196612
Sparse Core Ops, SparseCore 0:
  95.5 30.5 all-reduce.6
  129.9 92.6 all-reduce.4
  225.3 14.2 reduce-scatter.4
  243.2 106.9 reduce-scatter.2
  353.0 81.1 all-reduce.8
where the time goes:
time: 1050 us
  blocking collectives  752 us (72%)
  waiting for transfers between devices  216 us (21%)
  matrix products  57.5 us (5%)
  between operations  13.9 us (1%)
    psum x1, blocking collectives, body(): magnitude_grad = lax.psum(mag_part, ('dp', 'row'))  681 us
    reduce_scatter x1, waiting for transfers between devices, body(): pre_rows = lax.psum_scatter(term, 'row', scatter_dimension=0, tiled=True)  109 us
    psum x1, waiting for transfers between devices, body(): projected = lax.psum(proj_part, 'row')  94.7 us
    psum x1, blocking collectives, body(): column_square = lax.psum(jnp.sum(adapted * adapted, axis=0), 'row')  70.5 us
  transfers between devices with their start and end apart: 5, of which 4 were waited for; matrix products, arithmetic and copies ran while one was open for 4% of the time, Pallas kernels for 0%

commit v1 on v0

v1 whole, which is shorter than its diff:
```python
import functools

import jax
import jax.numpy as jnp
from jax import lax
from jax.experimental import pallas as pl
from jax.experimental.pallas import tpu as pltpu
from jax.sharding import PartitionSpec as P

MESH = pl.DeviceIdType.MESH
F32 = jnp.float32
BF16 = jnp.bfloat16
CHUNKS = 8
SIDE = 4
DEPTH = 8


def wrap(value, size):
    return lax.rem(value, size)


def kernel(
    x_ref, f_hbm, b_ref, a_ref, g_ref, c_hbm,
    mixed_ref, ig_ref, ag_ref, bg_ref, mg_ref, sc_ref,
    fro, cot, part, s1r, s2r, sums, s3r, s4r,
    nx, ny, mx, my, mz, norm,
    prs, prx, pry, prg, pbf,
    asend, arecv, agf,
    iga, igr, upacc, ups, upr, bs, br, bg,
    fsem, csem,
    s1s, s1q, s2s, s2q, s3s, s3q, s4s, s4q,
    nxs, nxq, nys, nyq, mxs, mxq, mys, myq, mzs, mzq,
    p1s, p1q, p2s, p2q, p3s, p3q,
    ars, arq, azs, azq, axs, axq, ays, ayq,
    sib_s, sib_q, brs, brq, bgs, bgq,
):
    W = fro.shape[2]
    r = lax.axis_index("row")
    z = lax.axis_index("dp")
    k = lax.axis_index("col")
    x = lax.rem(r, SIDE)
    y = lax.div(r, SIDE)

    def at_x(p):
        return {"row": y * SIDE + p}

    def at_y(p):
        return {"row": p * SIDE + x}

    def at_z(p):
        return {"dp": p}

    sibling = {"col": 1 - k}
    first = ((x, at_x), (y, at_y))
    second = ((y, at_y), (x, at_x))

    def cols(c):
        return pl.ds(pl.multiple_of(c * W, 128), W)

    def rcopy(src, dst, ss, rs, dev):
        return pltpu.make_async_remote_copy(
            src_ref=src, dst_ref=dst, send_sem=ss, recv_sem=rs,
            device_id=dev, device_id_type=MESH,
        )

    def f_copy(c):
        return pltpu.make_async_copy(f_hbm.at[:, cols(c)], fro.at[c], fsem.at[c])

    def c_copy(c):
        return pltpu.make_async_copy(c_hbm.at[:, cols(c)], cot.at[c], csem.at[c])

    def near(pos, d):
        return wrap(pos + (1 if d == 0 else SIDE - 1), SIDE)

    def s1(kind, c, d):
        pos, dev = first[kind]
        return rcopy(
            part.at[c, wrap(pos + 2, SIDE), pl.ds(2 * d, 2)], s1r.at[c, d],
            s1s.at[c, d], s1q.at[c, d], dev(near(pos, d)),
        )

    def s2(kind, c, d):
        pos, dev = first[kind]
        return rcopy(
            part.at[c, near(pos, d)], s2r.at[c, d],
            s2s.at[c, d], s2q.at[c, d], dev(near(pos, d)),
        )

    def s3(kind, c, d):
        pos, dev = second[kind]
        return rcopy(
            sums.at[c, wrap(pos + 2, SIDE), pl.ds(16 * d, 16)], s3r.at[c, d],
            s3s.at[c, d], s3q.at[c, d], dev(near(pos, d)),
        )

    def s4(kind, c, d):
        pos, dev = second[kind]
        return rcopy(
            sums.at[c, near(pos, d)], s4r.at[c, d],
            s4s.at[c, d], s4q.at[c, d], dev(near(pos, d)),
        )

    def t1(i):
        for kind in (0, 1):
            for d in (0, 1):
                s1(kind, 2 * i + kind, d).start()

    def t2(i):
        for kind in (0, 1):
            c = 2 * i + kind
            pos, _ = first[kind]
            for d in (0, 1):
                s1(kind, c, d).wait_recv()
                nb = near(pos, d)
                rows = pl.ds(2 * d, 2)
                part[c, nb, rows] = (
                    part[c, nb, rows].astype(F32) + s1r[c, d].astype(F32)
                ).astype(BF16)
                s2(kind, c, d).start()

    def t3(i):
        for kind in (0, 1):
            c = 2 * i + kind
            pos, _ = first[kind]
            for d in (0, 1):
                s2(kind, c, d).wait_recv()
            for j in range(SIDE):
                sums[c, j] = (
                    part[c, pos, j].astype(F32) + s2r[c, 0, j].astype(F32)
                    + s2r[c, 1, j].astype(F32)
                ).astype(BF16)
            for d in (0, 1):
                s3(kind, c, d).start()

    def t4(i):
        for kind in (0, 1):
            c = 2 * i + kind
            pos, _ = second[kind]
            for d in (0, 1):
                s3(kind, c, d).wait_recv()
                nb = near(pos, d)
                rows = pl.ds(16 * d, 16)
                sums[c, nb, rows] = (
                    sums[c, nb, rows].astype(F32) + s3r[c, d].astype(F32)
                ).astype(BF16)
                s4(kind, c, d).start()

    def t5(i):
        for kind in (0, 1):
            c = 2 * i + kind
            pos, _ = first[kind]
            own, _ = second[kind]
            for d in (0, 1):
                s4(kind, c, d).wait_recv()
            pre = (
                part[c, pos, own].astype(F32) + s2r[c, 0, own].astype(F32)
                + s2r[c, 1, own].astype(F32)
                + s4r[c, 0].astype(F32) + s4r[c, 1].astype(F32)
            )
            mixed_ref[:, cols(c)] = (pre * sc_ref[pl.ds(c, 1), :]).astype(BF16)

    def gather(buf, pos, size, dev, ss, rs):
        return [
            rcopy(buf.at[pos], buf.at[pos], ss.at[d], rs.at[d], dev(wrap(pos + d, size)))
            for d in range(1, size)
        ]

    norm_x = gather(nx, x, SIDE, at_x, nxs, nxq)
    norm_y = gather(ny, y, SIDE, at_y, nys, nyq)
    mag_x = gather(mx, x, SIDE, at_x, mxs, mxq)
    mag_y = gather(my, y, SIDE, at_y, mys, myq)
    mag_z = gather(mz, z, DEPTH, at_z, mzs, mzq)
    proj_x = [
        rcopy(prs.at[wrap(x + d, SIDE)], prx.at[x], p1s.at[d], p1q.at[d], at_x(wrap(x + d, SIDE)))
        for d in range(1, SIDE)
    ]
    proj_y = gather(pry, y, SIDE, at_y, p2s, p2q)
    proj_g = gather(prg, x, SIDE, at_x, p3s, p3q)
    a_part = [
        rcopy(asend.at[wrap(z + d, DEPTH)], arecv.at[z], ars.at[d], arq.at[d], at_z(wrap(z + d, DEPTH)))
        for d in range(1, DEPTH)
    ]
    kz = lax.rem(z, 2)
    iz = lax.div(z, 2)
    pz = x + kz * (y - x)
    a_z = [
        rcopy(agf.at[kz, pz, iz], agf.at[kz, pz, iz], azs.at[d], azq.at[d], at_z(wrap(z + d, DEPTH)))
        for d in range(1, DEPTH)
    ]
    a_x = gather(agf.at[0], x, SIDE, at_x, axs, axq)
    a_y = gather(agf.at[1], y, SIDE, at_y, ays, ayq)
    b_part = [
        rcopy(bs.at[wrap(z + d, DEPTH)], br.at[z], brs.at[d], brq.at[d], at_z(wrap(z + d, DEPTH)))
        for d in range(1, DEPTH)
    ]
    b_z = gather(bg, z, DEPTH, at_z, bgs, bgq)
    up_x = rcopy(ups, upr, sib_s.at[0], sib_q.at[0], sibling)
    ig_x = rcopy(iga.at[1 - k], igr, sib_s.at[1], sib_q.at[1], sibling)

    def start(copies):
        for copy in copies:
            copy.start()

    def wait(copies):
        for copy in copies:
            copy.wait_recv()

    def total(buf, count):
        value = buf[0].astype(F32)
        for j in range(1, count):
            value = value + buf[j].astype(F32)
        return value

    for c in (0, 1):
        f_copy(c).start()
    for c in (0, 1):
        c_copy(c).start()

    @pl.loop(2, CHUNKS)
    def _(c):
        f_copy(c).start()

    @pl.loop(2, CHUNKS)
    def _(c):
        c_copy(c).start()

    barrier = pltpu.get_barrier_semaphore()
    for d in range(1, SIDE):
        for dev in (at_x(wrap(x + d, SIDE)), at_y(wrap(y + d, SIDE))):
            pl.semaphore_signal(barrier, inc=1, device_id=dev, device_id_type=MESH)
    for d in range(1, DEPTH):
        pl.semaphore_signal(barrier, inc=1, device_id=at_z(wrap(z + d, DEPTH)), device_id_type=MESH)
    pl.semaphore_signal(barrier, inc=1, device_id=sibling, device_id_type=MESH)

    low = jnp.dot(x_ref[...], b_ref[...], preferred_element_type=F32).T
    for q in range(SIDE):
        prs[q] = low[:, 128 * q:128 * (q + 1)]
    prx[x] = prs[x]

    def adapt(c):
        f_copy(c).wait()
        square = jnp.zeros((1, W), F32)
        for kb in range(4):
            rows = pl.ds(128 * kb, 128)
            value = fro[c, rows, :].astype(F32) + jnp.dot(
                b_ref[rows, :], a_ref[:, cols(c)], preferred_element_type=F32
            )
            square = square + jnp.sum(value * value, axis=0, keepdims=True)
            fro[c, rows, :] = value.astype(BF16)
        nx[x, pl.ds(c, 1), :] = square

    def products(i):
        for kind in (0, 1):
            c = 2 * i + kind
            c_copy(c).wait()
            value = jnp.dot(x_ref[...], fro[c], preferred_element_type=F32)
            mx[x, pl.ds(c, 1), :] = jnp.sum(
                value * cot[c].astype(F32), axis=0, keepdims=True
            )
            low = value.astype(BF16)
            for yy in range(SIDE):
                for xx in range(SIDE):
                    t = 32 * (SIDE * yy + xx)
                    where = (c, xx, yy) if kind == 0 else (c, yy, xx)
                    part[where] = low[t:t + 32]

    adapt(0)
    adapt(1)
    products(0)
    pl.semaphore_wait(barrier, 2 * (SIDE - 1) + DEPTH)
    start(proj_x)
    t1(0)

    @pl.loop(2, CHUNKS)
    def _(c):
        adapt(c)

    start(norm_x)

    @pl.loop(1, 4)
    def _(i):
        products(i)
        t1(i)

        @pl.when(i == 1)
        def _():
            wait(proj_x)
            pry[y] = total(prx, SIDE)
            start(proj_y)
            wait(norm_x)
            ny[y] = total(nx, SIDE)
            start(norm_y)

        @pl.when(i == 2)
        def _():
            wait(proj_y)
            prg[x] = total(pry, SIDE).astype(BF16)
            start(proj_g)
            wait(norm_y)
            size = jnp.sqrt(total(ny, SIDE) + 1e-06)
            norm[...] = size
            sc_ref[...] = g_ref[...] / size

        t2(i - 1)

    start(mag_x)
    wait(proj_g)
    for q in range(SIDE):
        for j in range(SIDE):
            pbf[j, :, 128 * q:128 * (q + 1)] = prg[q, 16 * j:16 * (j + 1), :]

    @pl.loop(0, 4)
    def _(i):
        for kind in (0, 1):
            c = 2 * i + kind
            pos, _ = first[kind]
            asend[c] = jnp.dot(pbf[pos], cot[c], preferred_element_type=F32).astype(BF16)

    start(a_part)
    arecv[z] = asend[z]
    t2(3)
    wait(mag_x)
    my[y] = total(mx, SIDE)
    start(mag_y)
    t3(0)

    iga[...] = jnp.zeros_like(iga)
    upacc[...] = jnp.zeros_like(upacc)

    contract = (((1,), (1,)), ((), ()))

    def grads(c):
        grad = (cot[c].astype(F32) * sc_ref[pl.ds(c, 1), :]).astype(BF16)
        for h in (0, 1):
            iga[h] += lax.dot_general(
                grad, fro[c, pl.ds(256 * h, 256), :], contract, preferred_element_type=F32
            )
        upacc[...] += lax.dot_general(
            grad, a_ref[:, cols(c)], contract, preferred_element_type=F32
        )

    @pl.loop(0, 4)
    def _(i):
        @pl.loop(0, 2)
        def _(kind):
            grads(2 * i + kind)

        @pl.when(i == 0)
        def _():
            wait(a_part)
            agf[kz, pz, iz] = total(arecv, DEPTH).astype(BF16)
            start(a_z)
            wait(mag_y)
            mz[z] = total(my, SIDE)
            start(mag_z)

        @pl.when(i == 2)
        def _():
            wait(a_z)
            start(a_x)
            start(a_y)

        @pl.when(i < 3)
        def _():
            t3(i + 1)

        @pl.when(i == 3)
        def _():
            ups[...] = upacc[...].astype(BF16)
            up_x.start()
            ig_x.start()

        t4(i)

    up_x.wait_recv()
    up = (ups[...].astype(F32) + upr[...].astype(F32)).astype(BF16)
    bt = lax.dot_general(up, x_ref[...], (((0,), (0,)), ((), ())), preferred_element_type=F32)
    for j in range(DEPTH):
        bs[j] = bt[8 * j:8 * (j + 1), :]
    br[z] = bs[z]
    start(b_part)

    @pl.loop(0, 2)
    def _(i):
        t5(i)

    ig_x.wait_recv()
    ig_ref[...] = (iga[k] + igr[...]).astype(BF16)
    wait(b_part)
    bg[z] = total(br, DEPTH)
    start(b_z)

    @pl.loop(2, 4)
    def _(i):
        t5(i)

    wait(a_x)
    wait(a_y)
    for kind in (0, 1):
        for j in range(SIDE):
            for i in range(4):
                ag_ref[16 * j:16 * (j + 1), W * (2 * i + kind):W * (2 * i + kind + 1)] = agf[kind, j, i]
    wait(mag_z)
    mg_ref[...] = total(mz, DEPTH) / norm[...]
    wait(b_z)
    for j in range(DEPTH):
        bg_ref[8 * j:8 * (j + 1), :] = bg[j]

    @pl.loop(0, 4)
    def _(i):
        for kind in (0, 1):
            for d in (0, 1):
                for send in (s1, s2, s3, s4):
                    send(kind, 2 * i + kind, d).wait_send()

    for copies in (
        norm_x, norm_y, mag_x, mag_y, mag_z, proj_x, proj_y, proj_g,
        a_part, a_z, a_x, a_y, b_part, b_z, [up_x, ig_x],
    ):
        for copy in copies:
            copy.wait_send()


def body(inputs, frozen, factor_b, factor_a, magnitude, cotangent):
    tokens, depth = inputs.shape
    width = frozen.shape[1]
    rank = factor_a.shape[0]
    W = width // CHUNKS
    share = tokens // (SIDE * SIDE)
    quarter = tokens // SIDE
    dma = pltpu.SemaphoreType.DMA
    scratch = [
        pltpu.VMEM((CHUNKS, depth, W), BF16),
        pltpu.VMEM((CHUNKS, tokens, W), BF16),
        pltpu.VMEM((CHUNKS, SIDE, SIDE, share, W), BF16),
        pltpu.VMEM((CHUNKS, 2, 2, share, W), BF16),
        pltpu.VMEM((CHUNKS, 2, SIDE, share, W), BF16),
        pltpu.VMEM((CHUNKS, SIDE, share, W), BF16),
        pltpu.VMEM((CHUNKS, 2, share // 2, W), BF16),
        pltpu.VMEM((CHUNKS, 2, share, W), BF16),
        pltpu.VMEM((SIDE, CHUNKS, W), F32),
        pltpu.VMEM((SIDE, CHUNKS, W), F32),
        pltpu.VMEM((SIDE, CHUNKS, W), F32),
        pltpu.VMEM((SIDE, CHUNKS, W), F32),
        pltpu.VMEM((DEPTH, CHUNKS, W), F32),
        pltpu.VMEM((CHUNKS, W), F32),
        pltpu.VMEM((SIDE, rank, quarter), F32),
        pltpu.VMEM((SIDE, rank, quarter), F32),
        pltpu.VMEM((SIDE, rank, quarter), F32),
        pltpu.VMEM((SIDE, rank, quarter), BF16),
        pltpu.VMEM((SIDE, rank // SIDE, tokens), BF16),
        pltpu.VMEM((CHUNKS, rank // SIDE, W), BF16),
        pltpu.VMEM((DEPTH, rank // SIDE, W), BF16),
        pltpu.VMEM((2, SIDE, CHUNKS // 2, rank // SIDE, W), BF16),
        pltpu.VMEM((2, tokens, depth // 2), F32),
        pltpu.VMEM((tokens, depth // 2), F32),
        pltpu.VMEM((tokens, rank), F32),
        pltpu.VMEM((tokens, rank), BF16),
        pltpu.VMEM((tokens, rank), BF16),
        pltpu.VMEM((DEPTH, rank // DEPTH, depth), F32),
        pltpu.VMEM((DEPTH, rank // DEPTH, depth), F32),
        pltpu.VMEM((DEPTH, rank // DEPTH, depth), F32),
        dma((CHUNKS,)), dma((CHUNKS,)),
    ]
    scratch += [dma((CHUNKS, 2))] * 8
    scratch += [dma((SIDE,))] * 8 + [dma((DEPTH,))] * 2
    scratch += [dma((SIDE,))] * 6
    scratch += [dma((DEPTH,))] * 4 + [dma((SIDE,))] * 4
    scratch += [dma((2,))] * 2 + [dma((DEPTH,))] * 4
    vmem = pl.BlockSpec(memory_space=pltpu.VMEM)
    hbm = pl.BlockSpec(memory_space=pl.ANY)
    mixed, ig, ag, bt, mg, scale = pl.pallas_call(
        kernel,
        out_shape=(
            jax.ShapeDtypeStruct((share, width), BF16),
            jax.ShapeDtypeStruct((tokens, depth // 2), BF16),
            jax.ShapeDtypeStruct((rank, width), BF16),
            jax.ShapeDtypeStruct((rank, depth), F32),
            jax.ShapeDtypeStruct((CHUNKS, W), F32),
            jax.ShapeDtypeStruct((CHUNKS, W), F32),
        ),
        in_specs=[vmem, hbm, vmem, vmem, vmem, hbm],
        out_specs=(vmem,) * 6,
        scratch_shapes=scratch,
        compiler_params=pltpu.CompilerParams(
            collective_id=0, has_side_effects=True, vmem_limit_bytes=60 * 1024 * 1024
        ),
    )(inputs, frozen, factor_b, factor_a, magnitude.reshape(CHUNKS, W), cotangent)
    a_grad = ag.astype(F32) * scale.reshape(1, width)
    return (mixed, ig, a_grad, bt.T, mg.reshape(width))


def solution(mesh):
    return jax.shard_map(
        body,
        mesh=mesh,
        in_specs=(
            P("dp", "row"),
            P("row", "col"),
            P("row", None),
            P(None, "col"),
            P("col"),
            P("dp", "col"),
        ),
        out_specs=(
            P(("dp", "row"), "col"),
            P("dp", ("row", "col")),
            P(None, "col"),
            P("row", None),
            P("col"),
        ),
        check_vma=False,
    )
```

time: 1050 us -> 87.8 us (0.08)
  blocking collectives: 752 us -> 0 us
  waiting for transfers between devices: 216 us -> 0 us
  Pallas kernels: 0 us -> 77 us
  matrix products: 57.5 us -> 0 us
  between operations: 13.9 us -> 0.65 us
    psum x2 -> x0, blocking collectives: 752 us -> none  [the longest x1 681 us: body(): magnitude_grad = lax.psum(mag_part, ('dp', 'row'))]
    reduce_scatter x2 -> x0, waiting for transfers between devices: 113 us -> none  [the longest x1 109 us: body(): pre_rows = lax.psum_scatter(term, 'row', scatter_dimension=0, tiled=True)]
    psum x3 -> x0, waiting for transfers between devices: 104 us -> none  [the longest x1 94.7 us: body(): projected = lax.psum(proj_part, 'row')]
    pallas_call x0 -> x1, Pallas kernels: none -> 77 us  [body(): pl.pallas_call(kernel, out_shape=(jax.ShapeDtypeStruct((share, width), BF...]
    dot_general x9 -> x0, matrix products: 57.5 us -> none  [the longest x1 12.8 us: body(): a_part = jnp.dot(projected.T, grad_pre, precision=highest)]
  transfers between devices with their start and end apart: 5 -> 0, of which waited for: 4 -> 0; matrix products, arithmetic and copies ran while one was open for 4% -> 0% of each run, Pallas kernels for 0% -> 0%
where the time goes in v1:
time: 87.8 us; the launch traced here: 87.5 us
  Pallas kernels  77 us (88%)
  local copies, waits for them, and re-layouts  7.26 us (8%)
  other arithmetic  2.61 us (3%)
    pallas_call x1, Pallas kernels, body(): pl.pallas_call(kernel, out_shape=(jax.ShapeDtypeStruct((share, width), BF...  77 us
    unnamed x10, local copies, waits for them, and re-layouts  3.73 us
    mul x1, other arithmetic, body(): a_grad = ag.astype(F32) * scale.reshape(1, width)  2.61 us

profile of v1, /device:TPU:4, one launch (start us, length us, event | category | flops | bytes accessed | tf_op | source)
XLA Modules:
  0.0 87.5 jit_solution(9080428206176763665)
XLA Ops:
  0.6 1.4 %reshape.18.g_ref = f32[8,896]{1,0:T(8,128)} reshape(f32[7168]{0:T(1024)} %param.10) | data formatting | bytes 57344 | tf_op jit(solution)/shard_map/reshape | solution.py:488
  2.0 1.6 %copy.11.b_ref = bf16[512,64]{1,0:T(8,128)(2,1)} copy(bf16[512,64]{0,1:T(8,128)(2,1)} %param.8) | data formatting | bytes 131072 | tf_op args[2]
  3.6 77.0 %shard_map.101 = (bf16[32,7168]{1,0:T(8,128)(2,1)}, bf16[512,256]{1,0:T(8,128)(2,1)}, bf16[64,7168]{1,0:T(8,128)(2,1)}, f32[64,512]{1,0:T(8,128)}, f32[8,896]{1,0:T(8,128)}, /*index=5*/f32[8,896]{1,0:T(8,128)}) custom-call(bf16[512,512]{1,0:T(8,128)(2,1)} %x_ref.1, bf16[512,7168]{1,0:T(8,128)(2,1)} %f_hbm.1, bf16[512,64]{1,0:T(8,128)(2,1)} %copy.11.b_ref, ...), custom_call_target="tpu_custom_call" | custom-call | tf_op jit(solution)/shard_map/pallas_call | solution.py:472
  80.6 0.0 copy-start
  80.6 0.8 mul.10
  81.4 1.4 %reshape.19 = f32[7168]{0:T(1024)} reshape(f32[8,896]{1,0:T(8,128)} %get-tuple-element.16) | data formatting | bytes 57344 | tf_op jit(solution)/shard_map/reshape | solution.py:490
  82.8 0.0 copy-start.1
  82.8 0.0 copy-start.2
  82.8 2.6 %convert_multiply_fusion = f32[64,7168]{1,0:T(8,128)} fusion(bf16[64,7168]{1,0:T(8,128)(2,1)} %get-tuple-element.13, f32[7168]{0:T(1024)S(1)} %mul.10), kind=kLoop, calls=%fused_computation | loop fusion | flops 917504 | bytes 2781184 | tf_op jit(solution)/shard_map/mul | solution.py:489
  85.4 0.0 copy-done
  85.4 0.8 copy.15
  86.1 0.0 copy-done.1
  86.1 0.7 copy.16
  86.8 0.0 copy-done.2
  86.8 0.7 copy.17
Async XLA Ops:
  80.6 4.8 %copy-start = (bf16[32,7168]{1,0:T(8,128)(2,1)S(1)}, bf16[32,7168]{1,0:T(8,128)(2,1)}, u32[]{:S(2)}) copy-start(bf16[32,7168]{1,0:T(8,128)(2,1)} %get-tuple-element.22) | copy-start | bytes 1376260
  82.8 3.4 %copy-start.1 = (bf16[512,256]{1,0:T(8,128)(2,1)S(1)}, bf16[512,256]{1,0:T(8,128)(2,1)}, u32[]{:S(2)}) copy-start(bf16[512,256]{1,0:T(8,128)(2,1)} %get-tuple-element.23) | copy-start | bytes 786436
  82.8 4.1 %copy-start.2 = (f32[64,512]{1,0:T(8,128)S(1)}, f32[64,512]{1,0:T(8,128)}, u32[]{:S(2)}) copy-start(f32[64,512]{1,0:T(8,128)} %get-tuple-element.15) | copy-start | bytes 393220
